TPU v7x, 32 devices: a whole 2x2x4 slice. The times are simulated.
32 devices in a mesh: parts: 2 (over y), docs: 4 (over z), heads: 2 (over x), sub: 2 (over core).
Axes of the slice: x: 2, y: 2, z: 4, core: 2. Of those that a mesh axis runs over, the one named last changes fastest.
Arguments:
- hidden_rows: bfloat16 [16, 128, 8192], P(('parts', 'docs'), None, ('heads', 'sub')), parts along dimension 0, may hold values from -4200 to 4200
- norm_gain: bfloat16 [8192], P(('heads', 'sub')), may hold values from 0.099609375 to 1.8984375
- key_weight: bfloat16 [8192, 512], P(('heads', 'sub')), may hold values from -0.0625 to 0.0625
- value_weight: bfloat16 [8192, 512], P(('heads', 'sub')), may hold values from -0.0625 to 0.0625
- recompute_block: int32 [16], P(('parts', 'docs')), parts along dimension 0, may hold values from 0 to 3
- cache_keys: bfloat16 [16, 512, 512], P(('parts', 'docs'), 'sub', 'heads'), parts along dimension 0, may hold values from -6 to 6
- cache_values: bfloat16 [16, 512, 512], P(('parts', 'docs'), 'sub', 'heads'), parts along dimension 0, may hold values from -6 to 6
- slot_of_doc: int32 [16], P('parts'), parts along dimension 0, may hold values from 0 to 7, as said below
- session_docs: int32 [8, 3], P('parts'), parts along dimension 0, may hold values from -1 to 7, as said below
- session_count: int32 [8], P('parts'), parts along dimension 0, may hold values from 1 to 3, as said below
- turn_queries: bfloat16 [8, 128, 4096], P(('parts', 'docs'), None, 'heads'), parts along dimension 0, may hold values from -170 to 170
- turn_keys: bfloat16 [8, 128, 512], P(('parts', 'docs'), 'sub', 'heads'), parts along dimension 0, may hold values from -6 to 6
- turn_values: bfloat16 [8, 128, 512], P(('parts', 'docs'), 'sub', 'heads'), parts along dimension 0, may hold values from -6 to 6
- turn_length: int32 [8], P(('parts', 'docs')), parts along dimension 0, may hold values from 32 to 128, as said below
Outputs:
- attended: bfloat16 [8, 128, 4096], P(('parts', 'docs'), 'sub', 'heads'), parts along dimension 0
There are 2 independent parts, one for each index of `parts`. A program takes and returns all parts, laid end to end along the dimension named above; an argument that names none is the same for every part. Nothing has to cross between parts.
Inputs may be any that keep to these rules, and one draw needn't show every extreme that they name: `session_docs`: row e lists session e's documents in its first session_count[e] entries and -1 after them; one session's documents are distinct and their slots slot_of_doc[doc] lie on distinct indices of docs (slot // 2). `session_count`: some session has exactly 3 documents and some exactly 1. `slot_of_doc`: a permutation; a document's cache rows, hidden rows and block index stand at its slot. `turn_length`: some session has exactly 128 tokens and some exactly 32.
All inputs are finite; a program needn't handle non-finite values.
Results may differ from a plain program's by a relative error of at most 0.012.
Values may be sent and summed in bfloat16 or wider, within the bound.
A program may use at most 64 MiB of HBM per device.

v0:
```python
import jax
import jax.numpy as jnp
from jax import lax
from jax.sharding import PartitionSpec as P

D = 8192
HD = 128
BLK = 128
QLEN = 128
GQA = 8


EPSILON = 1e-05
ROPE_BASE = 500000.0
NEGATIVE = -1e30


def rotate(values, positions):
    half_dim = values.shape[-1] // 2
    exponent = jnp.arange(half_dim, dtype=jnp.float32) * (2.0 / values.shape[-1])
    frequency = ROPE_BASE ** (-exponent)
    angles = positions.astype(jnp.float32)[..., None, None] * frequency
    cos_part = jnp.cos(angles)
    sin_part = jnp.sin(angles)
    first_half = values[..., :half_dim]
    second_half = values[..., half_dim:]
    return jnp.concatenate(
        [
            first_half * cos_part - second_half * sin_part,
            second_half * cos_part + first_half * sin_part,
        ],
        axis=-1,
    )


def attend(running, queries, key_rows, value_rows, allowed):
    run_max, run_sum, run_acc = running
    scores = jnp.einsum(
        "qhgd,khd->hgqk", queries, key_rows, preferred_element_type=jnp.float32
    ) * HD ** (-0.5)
    masked = jnp.where(allowed, scores, NEGATIVE)
    new_max = jnp.maximum(run_max, jnp.max(masked, axis=-1))
    weights = jnp.where(allowed, jnp.exp(scores - new_max[..., None]), 0.0)
    factor = jnp.exp(run_max - new_max)
    run_sum = run_sum * factor + jnp.sum(weights, axis=-1)
    update = jnp.einsum(
        "hgqk,khd->hgqd",
        weights.astype(jnp.bfloat16),
        value_rows,
        preferred_element_type=jnp.float32,
    )
    run_acc = run_acc * factor[..., None] + update
    return (new_max, run_sum, run_acc)


def split_page(one_page, kv_local):
    row_count = one_page.shape[0]
    key_rows = one_page[:, : kv_local * HD].reshape(row_count, kv_local, HD)
    value_rows = one_page[:, kv_local * HD :].reshape(row_count, kv_local, HD)
    return (key_rows, value_rows)


def local(
    hidden_rows,
    norm_gain,
    key_weight,
    value_weight,
    recompute_block,
    cache_keys,
    cache_values,
    slot_of_doc,
    session_docs,
    session_count,
    turn_queries,
    turn_keys,
    turn_values,
    turn_length,
):
    heads_here = lax.axis_size("heads")
    parts_sub = lax.axis_size("sub")
    half_index = lax.axis_index("sub")
    session = lax.axis_index("docs")
    docs_here, block_rows, local_width = hidden_rows.shape
    kv_local = cache_keys.shape[-1] // HD
    rows_half = block_rows // parts_sub
    half_rows = cache_keys.shape[1]
    docs_max = session_docs.shape[1]
    squares = jnp.sum(jnp.square(hidden_rows.astype(jnp.float32)), axis=-1)
    squares = lax.psum(squares, ("heads", "sub"))
    row_scale = lax.rsqrt(squares / D + EPSILON)
    scaled = (hidden_rows.astype(jnp.float32) * norm_gain.astype(jnp.float32)).astype(jnp.bfloat16)
    row_pieces = scaled.reshape(docs_here, parts_sub, rows_half, local_width)
    stacked_weights = jnp.stack(
        [
            key_weight.reshape(local_width, heads_here, kv_local * HD),
            value_weight.reshape(local_width, heads_here, kv_local * HD),
        ],
        axis=1,
    )
    partial_terms = jnp.einsum(
        "jsrd,dthc->hsjrtc", row_pieces, stacked_weights, preferred_element_type=jnp.float32
    )
    partial_terms = partial_terms.reshape(
        heads_here * parts_sub * docs_here * rows_half, 2 * kv_local * HD
    )
    own_rows = lax.psum_scatter(
        partial_terms.astype(jnp.bfloat16), ("heads", "sub"), scatter_dimension=0, tiled=True
    ).astype(jnp.float32)
    own_rows = own_rows.reshape(docs_here, rows_half, 2, kv_local, HD)
    own_scale = lax.dynamic_slice_in_dim(row_scale, half_index * rows_half, rows_half, 1)
    own_rows = own_rows * own_scale[:, :, None, None, None]
    row_ids = half_index * rows_half + jnp.arange(rows_half, dtype=jnp.int32)
    positions = recompute_block[:, None] * BLK + row_ids[None, :]
    new_keys = (
        rotate(own_rows[:, :, 0], positions)
        .astype(jnp.bfloat16)
        .reshape(docs_here, rows_half, kv_local * HD)
    )
    new_values = own_rows[:, :, 1].astype(jnp.bfloat16).reshape(docs_here, rows_half, kv_local * HD)
    fresh = jnp.concatenate([new_keys, new_values], axis=-1)
    fresh = lax.all_gather(fresh, "sub", axis=1, tiled=True)
    stored = jnp.concatenate([cache_keys, cache_values], axis=-1)
    global_rows = half_index * half_rows + jnp.arange(half_rows, dtype=jnp.int32)
    offsets = global_rows[None, :] - recompute_block[:, None] * BLK
    inside = (offsets >= 0) & (offsets < BLK)
    picks = jnp.clip(offsets, 0, BLK - 1)
    replaced = jax.vmap(lambda rows_of, row_picks: rows_of[row_picks])(fresh, picks)
    pages = jnp.where(inside[:, :, None], replaced, stored)
    my_docs = lax.dynamic_index_in_dim(session_docs, session, 0, keepdims=False)
    my_count = lax.dynamic_index_in_dim(session_count, session, 0, keepdims=False)
    in_list = jnp.arange(docs_max, dtype=jnp.int32) < my_count
    my_slots = jnp.where(in_list, slot_of_doc[jnp.where(in_list, my_docs, 0)], -1)
    length = turn_length[0]
    queries = turn_queries[0].reshape(QLEN, kv_local, GQA, HD)
    running = (
        jnp.full((kv_local, GQA, QLEN), NEGATIVE, jnp.float32),
        jnp.zeros((kv_local, GQA, QLEN), jnp.float32),
        jnp.zeros((kv_local, GQA, QLEN, HD), jnp.float32),
    )
    turn_rows = turn_keys.shape[1]
    key_ids = half_index * turn_rows + jnp.arange(turn_rows, dtype=jnp.int32)
    query_ids = jnp.arange(QLEN, dtype=jnp.int32)
    turn_seen = (key_ids[None, :] <= query_ids[:, None]) & (key_ids[None, :] < length)
    running = attend(
        running,
        queries,
        turn_keys[0].reshape(turn_rows, kv_local, HD),
        turn_values[0].reshape(turn_rows, kv_local, HD),
        turn_seen[None, None],
    )
    every_row = jnp.ones((1, 1, 1, half_rows), jnp.bool_)
    portion = lax.all_gather(pages, "docs", axis=0, tiled=True)

    def one_slot(position, inner_state):
        one_page = lax.dynamic_index_in_dim(portion, position, 0, keepdims=False)
        key_rows, value_rows = split_page(one_page, kv_local)
        wanted = jnp.any(my_slots == position)
        return lax.cond(
            wanted,
            lambda given: attend(given, queries, key_rows, value_rows, every_row),
            lambda given: given,
            inner_state,
        )

    running = lax.fori_loop(0, portion.shape[0], one_slot, running)
    run_max, run_sum, run_acc = running
    got_max, got_sum, got_acc = (
        lax.all_to_all(
            run_max.astype(jnp.bfloat16), "sub", split_axis=2, concat_axis=2, tiled=True
        ).astype(run_max.dtype),
        lax.all_to_all(
            run_sum.astype(jnp.bfloat16), "sub", split_axis=2, concat_axis=2, tiled=True
        ).astype(run_sum.dtype),
        lax.all_to_all(
            run_acc.astype(jnp.bfloat16), "sub", split_axis=2, concat_axis=2, tiled=True
        ).astype(run_acc.dtype),
    )
    query_half = QLEN // parts_sub
    got_max = got_max.reshape(kv_local, GQA, parts_sub, query_half)
    got_sum = got_sum.reshape(kv_local, GQA, parts_sub, query_half)
    got_acc = got_acc.reshape(kv_local, GQA, parts_sub, query_half, HD)
    joint_max = jnp.max(got_max, axis=2)
    source_weights = jnp.exp(got_max - joint_max[:, :, None, :])
    joint_sum = jnp.sum(got_sum * source_weights, axis=2)
    joint_acc = jnp.sum(got_acc * source_weights[..., None], axis=2)
    result = joint_acc / joint_sum[..., None]
    result = result.transpose(2, 0, 1, 3).reshape(query_half, kv_local * GQA * HD)
    own_queries = half_index * query_half + jnp.arange(query_half, dtype=jnp.int32)
    result = jnp.where(own_queries[:, None] < length, result, 0.0)
    return result.astype(jnp.bfloat16)[None]


def solution(mesh):
    in_specs = (
        P(("parts", "docs"), None, ("heads", "sub")),
        P(("heads", "sub")),
        P(("heads", "sub"), None),
        P(("heads", "sub"), None),
        P(("parts", "docs")),
        P(("parts", "docs"), "sub", "heads"),
        P(("parts", "docs"), "sub", "heads"),
        P("parts"),
        P("parts", None),
        P("parts"),
        P(("parts", "docs"), None, "heads"),
        P(("parts", "docs"), "sub", "heads"),
        P(("parts", "docs"), "sub", "heads"),
        P(("parts", "docs")),
    )
    out_specs = P(("parts", "docs"), "sub", "heads")
    return jax.shard_map(local, mesh=mesh, in_specs=in_specs, out_specs=out_specs, check_vma=False)
```

profile of v0, /device:TPU:0, one launch (start us, length us, event | category | flops | bytes accessed | tf_op | source)
XLA Modules:
  0.0 148.6 jit_solution(10817131984612177415)
XLA Ops:
  7.2 2.9 %copy.127 = bf16[2048,512]{0,1:T(8,128)(2,1)S(1)} copy(bf16[2048,512]{1,0:T(8,128)(2,1)} %param.20) | data formatting | bytes 4194304 | tf_op args[2]
  10.2 2.5 %copy.129 = bf16[2048,1,2,256]{3,0,2,1:T(8,128)(2,1)} copy(bf16[2048,1,2,256]{0,3,2,1:T(8,128)(2,1)S(1)} %bitcast.87) | data formatting | bytes 4194304 | tf_op jit(solution)/shard_map/stack;reshape | solution.py:93
  12.7 2.9 %copy.128 = bf16[2048,512]{0,1:T(8,128)(2,1)S(1)} copy(bf16[2048,512]{1,0:T(8,128)(2,1)} %param.21) | data formatting | bytes 4194304 | tf_op args[3]
  15.6 2.5 %copy.130 = bf16[2048,1,2,256]{3,0,2,1:T(8,128)(2,1)} copy(bf16[2048,1,2,256]{0,3,2,1:T(8,128)(2,1)S(1)} %bitcast.88) | data formatting | bytes 4194304 | tf_op jit(solution)/shard_map/stack;reshape | solution.py:93
  18.5 1.2 copy-done.1
  19.7 2.8 %fusion.13 = bf16[2,2,2,64,2,256]{5,3,1,2,0,4:T(8,128)(2,1)S(1)} fusion(bf16[2,2,64,2048,1,1]{3,2,1,0,5,4:T(8,128)(2,1)S(1)} %bitcast.94, bf16[2048,1,2,256]{3,0,2,1:T(8,128)(2,1)} %copy.130, bf16[2048,1,2,256]{3,0,2,1:T(8,128)(2,1)S(1)} %copy-done.1), kind=kOutput, calls=%fused_computation.25 | convolution fusion | flops 1082392576 | bytes 5767168 | tf_op jit(solution)/shard_map/jsrd,dthc->hsjrtc/dot_general | solution.py:100
  24.2 8.3 %psum.7 = f32[2,128]{1,0:T(2,128)S(1)} all-reduce(f32[2,128]{1,0:T(2,128)S(1)} %get-tuple-element.258), channel_id=1, replica_groups=mesh['parts'=2,'docs'=4,'heads'=2,'sub'=2] {'heads','sub'}, use_global_device_ids=true, to_apply=%region_4.5 | all-reduce | flops 256 | bytes 2048 | tf_op jit(solution)/shard_map/psum | solution.py:89
  33.1 15.4 %reduce-scatter.2.cloned.1.call-done = bf16[128,512]{1,0:T(8,128)(2,1)} async-done(((bf16[512,512]{1,0:T(8,128)(2,1)}), bf16[128,512]{1,0:T(8,128)(2,1)}) %reduce-scatter.2.cloned.1.call-update) | async-done | bytes 131088 | tf_op jit(solution)/shard_map/reduce_scatter | solution.py:106
  48.5 1.1 reshape.325
  50.6 2.0 %all_gather.6 = bf16[2,128,512]{2,1,0:T(8,128)(2,1)S(1)} all-gather(bf16[2,64,512]{2,1,0:T(8,128)(2,1)S(1)} %pad_maximum_fusion), channel_id=1, replica_groups=mesh['parts'=2,'docs'=4,'heads'=2,'sub'=2] {'sub'}, dimensions={1}, use_global_device_ids=true | all-gather | bytes 393216 | tf_op jit(solution)/shard_map/all_gather | solution.py:121
  52.6 3.9 %gather_fusion.1 = bf16[512,512]{1,0:T(8,128)(2,1)S(1)} fusion(bf16[2,128,512]{2,1,0:T(8,128)(2,1)S(1)} %all_gather.6, s32[512]{0:T(512)S(1)} %bitcast.84), kind=kCustom, calls=%fused_computation.1 | custom fusion | bytes 1052672 | tf_op jit(solution)/shard_map/vmap()/gather | solution.py:127
  56.5 1.1 maximum_select_fusion
  59.5 1.3 fusion.29
  63.0 40.7 %all-gather.2.cloned.1.call-done = bf16[8,256,512]{2,1,0:T(8,128)(2,1)} async-done(((bf16[2,256,512]{2,1,0:T(8,128)(2,1)}), bf16[8,256,512]{2,1,0:T(8,128)(2,1)}) %all-gather.2.cloned.1.call-update) | async-done | bytes 2097168 | tf_op jit(solution)/shard_map/all_gather | solution.py:152
  103.7 3.9 %copy.132 = bf16[8,256,512]{1,2,0:T(8,128)(2,1)} copy(bf16[8,256,512]{2,1,0:T(8,128)(2,1)} %all-gather.2.cloned.1.call-done) | data formatting | bytes 4194304 | tf_op jit(solution)/shard_map/while | solution.py:165
  107.6 19.0 %while.17 = (s32[]{:T(128)}, f32[2,8,128]{2,1,0:T(8,128)S(1)}, f32[2,8,128]{2,1,0:T(8,128)S(1)}, f32[2,8,128,128]{3,2,1,0:T(8,128)S(1)}, s32[3]{0:T(128)S(1)}, /...) while((s32[]{:T(128)}, f32[2,8,128]{2,1,0:T(8,128)S(1)}, ...), condition=%wide.region_11.12_spmd, body=%wide.region_5.11_spmd.sunk | while | flops 273158144 | bytes 10354903 | solution.py:165
  108.9 2.9 %conditional.2 = ((f32[2,8,128]{2,1,0:T(8,128)S(1)}, f32[2,8,128]{2,1,0:T(8,128)S(1)}, f32[2,8,128,128]{3,2,1,0:T(8,128)S(1)})) conditional(s32[]{:T(128)} %convert_element_type.105, (f32[2,8,128]{2,1,0:T(8,128)S(1)}, f32[2,8,128]{2,1,0:T(8,128)S(1)}, f32[2,8,128,128]{3,2,1,0:T(8,128)S(1)}) %tuple.59, (s32[]{:T(128)}, ...), branch_computations={%region_7.7_spmd, %region_8.10_spmd} | conditional | flops 273158144 | bytes 10354724 | solution.py:158
  118.3 2.9 %conditional.2 = ((f32[2,8,128]{2,1,0:T(8,128)S(1)}, f32[2,8,128]{2,1,0:T(8,128)S(1)}, f32[2,8,128,128]{3,2,1,0:T(8,128)S(1)})) conditional(s32[]{:T(128)} %convert_element_type.105, (f32[2,8,128]{2,1,0:T(8,128)S(1)}, f32[2,8,128]{2,1,0:T(8,128)S(1)}, f32[2,8,128,128]{3,2,1,0:T(8,128)S(1)}) %tuple.59, (s32[]{:T(128)}, ...), branch_computations={%region_7.7_spmd, %region_8.10_spmd} | conditional | flops 273158144 | bytes 10354724 | solution.py:158
  118.3 1.0 dynamic-slice_bitcast_fusion
  123.7 2.9 %conditional.2 = ((f32[2,8,128]{2,1,0:T(8,128)S(1)}, f32[2,8,128]{2,1,0:T(8,128)S(1)}, f32[2,8,128,128]{3,2,1,0:T(8,128)S(1)})) conditional(s32[]{:T(128)} %convert_element_type.105, (f32[2,8,128]{2,1,0:T(8,128)S(1)}, f32[2,8,128]{2,1,0:T(8,128)S(1)}, f32[2,8,128,128]{3,2,1,0:T(8,128)S(1)}) %tuple.59, (s32[]{:T(128)}, ...), branch_computations={%region_7.7_spmd, %region_8.10_spmd} | conditional | flops 273158144 | bytes 10354724 | solution.py:158
  123.8 1.0 dynamic-slice_bitcast_fusion
  126.9 3.7 %all_to_all.15 = bf16[2,2,512]{2,1,0:T(2,128)(2,1)S(1)} all-to-all(bf16[2,2,512]{2,1,0:T(2,128)(2,1)S(1)} %reshape.355), channel_id=1, replica_groups=mesh['parts'=2,'docs'=4,'heads'=2,'sub'=2] {'sub'}, dimensions={0} | all-to-all | bytes 8192 | tf_op jit(solution)/shard_map/all_to_all | solution.py:168
  131.3 3.7 %all_to_all.16 = bf16[2,2,512]{2,1,0:T(2,128)(2,1)S(1)} all-to-all(bf16[2,2,512]{2,1,0:T(2,128)(2,1)S(1)} %reshape.353), channel_id=1, replica_groups=mesh['parts'=2,'docs'=4,'heads'=2,'sub'=2] {'sub'}, dimensions={0} | all-to-all | bytes 8192 | tf_op jit(solution)/shard_map/all_to_all | solution.py:171
  135.8 4.2 %all_to_all.17 = bf16[2,8,128,128]{3,1,0,2:T(8,128)(2,1)S(1)} all-to-all(bf16[2,8,128,128]{3,1,0,2:T(8,128)(2,1)S(1)} %copy.178), channel_id=1, replica_groups=mesh['parts'=2,'docs'=4,'heads'=2,'sub'=2] {'sub'}, dimensions={2} | all-to-all | bytes 1048576 | tf_op jit(solution)/shard_map/all_to_all | solution.py:174
  (118 shorter events, 22.7 us)
Async XLA Ops:
  6.5 54.3 %copy-start = (s32[8]{0:T(128)S(1)}, s32[8]{0:T(128)}, u32[]{:S(2)}) copy-start(s32[8]{0:T(128)} %param.25) | copy-start | bytes 100
  6.5 42.0 %reduce-scatter.2.cloned.1.call-start = ((), (), s32[]{:S(2)}) async-start(), calls=%async_computation.4 | async-start | bytes 655360 | tf_op jit(solution)/shard_map/reduce_scatter | solution.py:106
  15.6 2.5 %copy-start.2 = (bf16[2,128,2048]{2,1,0:T(8,128)(2,1)S(1)}, bf16[2,128,2048]{2,1,0:T(8,128)(2,1)}, u32[]{:S(2)}) copy-start(bf16[2,128,2048]{2,1,0:T(8,128)(2,1)} %param.18) | copy-start | bytes 3145732
  18.1 1.6 %copy-start.1 = (bf16[2048,1,2,256]{3,0,2,1:T(8,128)(2,1)S(1)}, bf16[2048,1,2,256]{3,0,2,1:T(8,128)(2,1)}, u32[]{:S(2)}) copy-start(bf16[2048,1,2,256]{3,0,2,1:T(8,128)(2,1)} %copy.129) | copy-start | bytes 6291460
  22.6 1.5 %copy-start.8 = (s32[2]{0:T(128)S(1)}, s32[2]{0:T(128)}, u32[]{:S(2)}) copy-start(s32[2]{0:T(128)} %param.22) | copy-start | bytes 28
  24.0 79.7 %all-gather.2.cloned.1.call-start = ((), (), s32[]{:S(2)}) async-start(), calls=%async_computation.5 | async-start | bytes 2621440 | tf_op jit(solution)/shard_map/all_gather | solution.py:152
  52.6 4.0 %copy-start.4 = (bf16[2,256,256]{2,1,0:T(8,128)(2,1)S(1)}, bf16[2,256,256]{2,1,0:T(8,128)(2,1)}, u32[]{:S(2)}) copy-start(bf16[2,256,256]{2,1,0:T(8,128)(2,1)} %param.24) | copy-start | bytes 786436
  52.6 4.0 %copy-start.5 = (bf16[2,256,256]{2,1,0:T(8,128)(2,1)S(1)}, bf16[2,256,256]{2,1,0:T(8,128)(2,1)}, u32[]{:S(2)}) copy-start(bf16[2,256,256]{2,1,0:T(8,128)(2,1)} %param.23) | copy-start | bytes 786436
  56.5 1.8 %copy-start.3 = (bf16[1,128,2048]{2,1,0:T(8,128)(2,1)S(1)}, bf16[1,128,2048]{2,1,0:T(8,128)(2,1)}, u32[]{:S(2)}) copy-start(bf16[1,128,2048]{2,1,0:T(8,128)(2,1)} %param.28) | copy-start | bytes 1572868
  56.5 2.1 %copy-start.6 = (bf16[1,64,256]{2,1,0:T(8,128)(2,1)S(1)}, bf16[1,64,256]{2,1,0:T(8,128)(2,1)}, u32[]{:S(2)}) copy-start(bf16[1,64,256]{2,1,0:T(8,128)(2,1)} %param.29) | copy-start | bytes 98308
  56.5 2.1 %copy-start.7 = (bf16[1,64,256]{2,1,0:T(8,128)(2,1)S(1)}, bf16[1,64,256]{2,1,0:T(8,128)(2,1)}, u32[]{:S(2)}) copy-start(bf16[1,64,256]{2,1,0:T(8,128)(2,1)} %param.30) | copy-start | bytes 98308
  56.5 2.4 %copy-start.9 = (s32[4]{0:T(128)S(1)}, s32[4]{0:T(128)}, u32[]{:S(2)}) copy-start(s32[4]{0:T(128)} %param.27) | copy-start | bytes 52
Sparse Core Ops, SparseCore 0:
  24.2 24.3 reduce-scatter.1
  57.7 45.9 all-gather.1
where the time goes:
time: 149 us
  waiting for transfers between devices  56.1 us (38%)
  local copies, waits for them, and re-layouts  29.4 us (20%)
  blocking collectives  21.9 us (15%)
  between operations  14.5 us (10%)
  other arithmetic  13.4 us (9%)
  matrix products  7.88 us (5%)
  loops' own time  5.44 us (4%)
    all_gather x1, waiting for transfers between devices, local(): portion = lax.all_gather(pages, 'docs', axis=0, tiled=True)  40.7 us
    reduce_scatter x1, waiting for transfers between devices, local(): lax.psum_scatter(partial_terms.astype(jnp.bfloat16), ('heads', 'sub'), sc...  15.4 us
    unnamed x29, local copies, waits for them, and re-layouts  8.73 us
    psum x1, blocking collectives, local(): squares = lax.psum(squares, ('heads', 'sub'))  8.34 us
    another operation x1, loops' own time, local(): running = lax.fori_loop(0, portion.shape[0], one_slot, running)  5.16 us
    reduce_or x8, other arithmetic, one_slot(): wanted = jnp.any(my_slots == position)  5.14 us
    another operation x2, local copies, waits for them, and re-layouts, local(): jnp.stack([key_weight.reshape(local_width, heads_here, kv_local * HD), va...  5.01 us
    while x3, local copies, waits for them, and re-layouts, local(): running = lax.fori_loop(0, portion.shape[0], one_slot, running)  4.83 us
  transfers between devices with their start and end apart: 2, of which 2 were waited for; matrix products, arithmetic and copies ran while one was open for 4% of the time, Pallas kernels for 0%

commit v1 on v0

--- a/solution.py
+++ b/solution.py
@@ -1,6 +1,9 @@
 import jax
 import jax.numpy as jnp
+import numpy as np
 from jax import lax
+from jax.experimental import pallas as pl
+from jax.experimental.pallas import tpu as pltpu
 from jax.sharding import PartitionSpec as P
 
 D = 8192
@@ -190,6 +193,391 @@
     return result.astype(jnp.bfloat16)[None]
 
 
+def fused_kernel(
+    docs_sm, count_sm, slot_sm, block_sm, length_sm,
+    hidden_hbm, gain_ref, kw_hbm, vw_hbm, ck_hbm, cv_hbm, cos_hbm, sin_hbm, tq_hbm, tk_hbm, tv_hbm,
+    out_ref,
+    hid, scaled, wbuf, own, oth, turn, stage, kv, stage_fresh, kv_fresh, fresh, cos_t, sin_t,
+    part_out, part_in, part_own, sq_out, sq_in, q_raw, q_all, run_max, run_sum, run_acc, o_send,
+    load_sem, w_sem, chip_send, chip_recv, a_send, a_recv, b_send, b_recv, f_send, f_recv,
+    p_send, p_recv, s_send, s_recv, o_sems,
+):
+    z = lax.axis_index("docs")
+    h = lax.axis_index("heads")
+    s = lax.axis_index("sub")
+    n_docs = 4
+    other = 1 - s
+    mesh_id = pl.DeviceIdType.MESH
+    pairs = [(1, 0), (1, 1), (0, 1), (0, 0)]
+
+    def lanes(start, size):
+        return pl.ds(pl.multiple_of(start, HD), size)
+
+    my_cols = lanes(s * HD, HD)
+    other_cols = lanes(other * HD, HD)
+
+    loads = [
+        (ck_hbm.at[:, :, my_cols], own.at[:, :, 0:HD]),
+        (cv_hbm.at[:, :, my_cols], own.at[:, :, HD : 2 * HD]),
+        (hidden_hbm, hid),
+        (tq_hbm.at[0, :, lanes(s * GQA * HD, GQA * HD)], q_raw),
+        (cos_hbm, cos_t),
+        (sin_hbm, sin_t),
+        (tk_hbm.at[0, :, my_cols], turn.at[s, :, 0:HD]),
+        (tv_hbm.at[0, :, my_cols], turn.at[s, :, HD : 2 * HD]),
+    ]
+    loads = [
+        pltpu.make_async_copy(src, dst, load_sem.at[i]) for i, (src, dst) in enumerate(loads)
+    ]
+    for i in (0, 1, 2):
+        loads[i].start()
+    w_loads = []
+    for i, (dh, ds) in enumerate(pairs):
+        head = 2 * lax.rem(h + dh, 2) + lax.rem(s + ds, 2)
+        cols = lanes(head * HD, HD)
+        w_loads.append(
+            [
+                pltpu.make_async_copy(kw_hbm.at[:, cols], wbuf.at[i, :, 0:HD], w_sem.at[2 * i]),
+                pltpu.make_async_copy(
+                    vw_hbm.at[:, cols], wbuf.at[i, :, HD : 2 * HD], w_sem.at[2 * i + 1]
+                ),
+            ]
+        )
+        for copy in w_loads[-1]:
+            copy.start()
+    for i in range(3, len(loads)):
+        loads[i].start()
+
+    barrier = pltpu.get_barrier_semaphore()
+    for dh, ds in pairs[:3]:
+        pl.semaphore_signal(
+            barrier, inc=1,
+            device_id={"heads": lax.rem(h + dh, 2), "sub": lax.rem(s + ds, 2)},
+            device_id_type=mesh_id,
+        )
+    for d in range(1, n_docs):
+        pl.semaphore_signal(
+            barrier, inc=1, device_id={"docs": lax.rem(z + d, n_docs)}, device_id_type=mesh_id
+        )
+    pl.semaphore_wait(barrier, 6)
+
+    def remote(src, dst, send, recv, device):
+        copy = pltpu.make_async_remote_copy(
+            src_ref=src, dst_ref=dst, send_sem=send, recv_sem=recv,
+            device_id=device, device_id_type=mesh_id,
+        )
+        copy.start()
+        return copy
+
+    partner = {"sub": other}
+    chip = [
+        remote(ck_hbm.at[:, :, other_cols], oth.at[:, :, 0:HD], chip_send.at[0], chip_recv.at[0], partner),
+        remote(cv_hbm.at[:, :, other_cols], oth.at[:, :, HD : 2 * HD], chip_send.at[1], chip_recv.at[1], partner),
+        remote(tk_hbm.at[0, :, other_cols], turn.at[s, :, 0:HD], chip_send.at[2], chip_recv.at[2], partner),
+        remote(tv_hbm.at[0, :, other_cols], turn.at[s, :, HD : 2 * HD], chip_send.at[3], chip_recv.at[3], partner),
+    ]
+
+    def reads(session, place):
+        flag = jnp.int32(0)
+        pick = jnp.int32(0)
+        for k in range(docs_sm.shape[1]):
+            listed = k < count_sm[session]
+            doc = docs_sm[session, k]
+            slot = jnp.int32(0)
+            for j in range(slot_sm.shape[0]):
+                slot = jnp.where(doc == j, slot_sm[j], slot)
+            local_slot = slot - 2 * place
+            hit = listed & (local_slot >= 0) & (local_slot < 2)
+            flag = jnp.where(hit, 1, flag)
+            pick = jnp.where(hit, local_slot, pick)
+        return flag, pick
+
+    picks = [reads(lax.rem(z + d, n_docs), z)[1] for d in range(n_docs)]
+    bias = []
+    for d in range(n_docs):
+        flag, _ = reads(z, lax.rem(z + n_docs - d, n_docs))
+        bias.append(jnp.where(flag == 1, jnp.float32(0.0), jnp.float32(NEGATIVE)))
+
+    def choose(index, blocks):
+        shape = blocks[0].shape
+        wide = [block.astype(jnp.float32) for block in blocks]
+        chosen = jnp.full(shape, index, jnp.int32)
+        result = wide[0]
+        for k in range(1, len(wide)):
+            result = jnp.where(chosen == k, wide[k], result)
+        return result.astype(blocks[0].dtype)
+
+    loads[0].wait()
+    loads[1].wait()
+    order = (2, 1, 3, 0)
+    holds, inner = [], []
+    for d in range(n_docs):
+        block = jnp.where(picks[d] == 1, block_sm[1], block_sm[0])
+        upper = jnp.where(block >= 2, 1, 0)
+        holds.append(upper == s)
+        inner.append(block - 2 * upper)
+    a_copies, b_copies, f_copies = {}, {}, {}
+    for d in order:
+        at = jnp.where(holds[d], 1 - inner[d], 0)
+        rows = choose(picks[d] * 2 + at, [own[j, c * BLK : (c + 1) * BLK, :] for j in range(2) for c in range(2)])
+        if d == 0:
+            kv[0, 0:BLK, :] = rows
+        else:
+            stage[d - 1, 0:BLK, :] = rows
+            a_copies[d] = remote(
+                stage.at[d - 1, 0:BLK], kv.at[d, 0:BLK], a_send.at[d - 1], a_recv.at[d - 1],
+                {"docs": lax.rem(z + d, n_docs)},
+            )
+    chip[0].wait_recv()
+    chip[1].wait_recv()
+    for d in order:
+        at = jnp.where(holds[d], 0, 1 - inner[d])
+        second = choose(picks[d] * 2 + at, [oth[j, c * BLK : (c + 1) * BLK, :] for j in range(2) for c in range(2)])
+        third = choose(
+            picks[d] * 2 + jnp.where(holds[d], 1, 0),
+            [half_rows[j, BLK : 2 * BLK, :] for j in range(2) for half_rows in (own, oth)],
+        )
+        if d == 0:
+            kv[0, BLK : 2 * BLK, :] = second
+            kv[0, 2 * BLK : 3 * BLK, :] = third
+        else:
+            stage[d - 1, BLK : 2 * BLK, :] = second
+            stage[d - 1, 2 * BLK : 3 * BLK, :] = third
+            b_copies[d] = remote(
+                stage.at[d - 1, BLK : 3 * BLK], kv.at[d, BLK : 3 * BLK],
+                b_send.at[d - 1], b_recv.at[d - 1], {"docs": lax.rem(z + d, n_docs)},
+            )
+
+    loads[2].wait()
+    width = hid.shape[-1]
+    gain = gain_ref[...].astype(jnp.float32)
+    sq_out[...] = jnp.zeros_like(sq_out)
+    for j in range(2):
+        total = jnp.zeros((BLK, HD), jnp.float32)
+        for c in range(width // HD):
+            cols = slice(c * HD, (c + 1) * HD)
+            x = hid[j, :, cols].astype(jnp.float32)
+            total = total + x * x
+            scaled[j * BLK : (j + 1) * BLK, cols] = (x * gain[:, cols]).astype(jnp.bfloat16)
+        sq_out[j : j + 1, :] = jnp.sum(total.T, axis=0, keepdims=True)
+    p_copies, s_copies = [], []
+    for i, (dh, ds) in enumerate(pairs):
+        for copy in w_loads[i]:
+            copy.wait()
+        device = {"heads": lax.rem(h + dh, 2), "sub": lax.rem(s + ds, 2)}
+        if i < 3:
+            s_copies.append(remote(sq_out, sq_in.at[i], s_send.at[i], s_recv.at[i], device))
+        term = jnp.dot(scaled[...], wbuf[i], preferred_element_type=jnp.float32)
+        if i < 3:
+            part_out[i] = term.astype(jnp.bfloat16)
+            p_copies.append(
+                remote(part_out.at[i], part_in.at[i], p_send.at[i], p_recv.at[i], device)
+            )
+        else:
+            part_own[...] = term
+
+    half = QLEN // 2
+    loads[3].wait()
+    for p in range(2):
+        for head in range(GQA):
+            at = (p * GQA + head) * half
+            q_all[at : at + half, :] = q_raw[p * half : (p + 1) * half, head * HD : (head + 1) * HD]
+    loads[6].wait()
+    loads[7].wait()
+    chip[2].wait_recv()
+    chip[3].wait_recv()
+    length = length_sm[0]
+    scale = HD ** (-0.5)
+    tile = 256
+
+    def scores_of(at, key_rows):
+        return lax.dot_general(
+            q_all[pl.ds(at, tile), :], key_rows, (((1,), (1,)), ((), ())),
+            preferred_element_type=jnp.float32,
+        ) * scale
+
+    def first(b, carry):
+        at = pl.multiple_of(b * tile, tile)
+        rows = turn[...].reshape(QLEN, 2 * HD)
+        scores = scores_of(at, rows[:, 0:HD])
+        row = lax.broadcasted_iota(jnp.int32, (tile, QLEN), 0)
+        query = (row & (half - 1)) + (b // 2) * half
+        key = lax.broadcasted_iota(jnp.int32, (tile, QLEN), 1)
+        seen = (key <= query) & (key < length)
+        scores = jnp.where(seen, scores, NEGATIVE)
+        top = jnp.max(scores, axis=-1, keepdims=True)
+        weights = jnp.exp(scores - top)
+        run_max[pl.ds(at, tile), :] = top
+        run_sum[pl.ds(at, tile), :] = jnp.sum(weights, axis=-1, keepdims=True)
+        run_acc[pl.ds(at, tile), :] = jnp.dot(
+            weights.astype(jnp.bfloat16), rows[:, HD : 2 * HD], preferred_element_type=jnp.float32
+        )
+        return carry
+
+    def step(at, key_rows, value_rows, added):
+        scores = scores_of(at, key_rows) + added
+        before = run_max[pl.ds(at, tile), :]
+        top = jnp.maximum(before, jnp.max(scores, axis=-1, keepdims=True))
+        weights = jnp.exp(scores - top)
+        factor = jnp.exp(before - top)
+        row_sum = run_sum[pl.ds(at, tile), :] * factor + jnp.sum(weights, axis=-1, keepdims=True)
+        acc = run_acc[pl.ds(at, tile), :] * factor + jnp.dot(
+            weights.astype(jnp.bfloat16), value_rows, preferred_element_type=jnp.float32
+        )
+        return top, row_sum, acc
+
+    def stored_step(d):
+        def body(b, carry):
+            at = pl.multiple_of(b * tile, tile)
+            top, row_sum, acc = step(at, kv[d, :, 0:HD], kv[d, :, HD : 2 * HD], bias[d])
+            run_max[pl.ds(at, tile), :] = top
+            run_sum[pl.ds(at, tile), :] = row_sum
+            run_acc[pl.ds(at, tile), :] = acc
+            return carry
+
+        lax.fori_loop(0, q_all.shape[0] // tile, body, 0)
+
+    lax.fori_loop(0, q_all.shape[0] // tile, first, 0)
+    stored_step(0)
+
+    loads[4].wait()
+    loads[5].wait()
+    for copy in s_copies:
+        copy.wait_recv()
+    for copy in p_copies:
+        copy.wait_recv()
+    squares = sq_out[...]
+    for i in range(3):
+        squares = squares + sq_in[i]
+    row_scale = lax.rsqrt(squares / D + EPSILON)
+    for j in range(2):
+        rows = slice(j * BLK, (j + 1) * BLK)
+        term = part_own[rows, :]
+        for i in range(3):
+            term = term + part_in[i, rows, :].astype(jnp.float32)
+        factor = jnp.broadcast_to(row_scale[j : j + 1, :], (BLK, HD)).T
+        keys = term[:, 0:HD] * factor
+        cos_rows = choose(block_sm[j], [cos_t[k * BLK : (k + 1) * BLK, :] for k in range(4)])
+        sin_rows = choose(block_sm[j], [sin_t[k * BLK : (k + 1) * BLK, :] for k in range(4)])
+        turned = keys * cos_rows + pltpu.roll(keys, HD // 2, 1) * sin_rows
+        fresh[j, :, 0:HD] = turned.astype(jnp.bfloat16)
+        fresh[j, :, HD : 2 * HD] = (term[:, HD : 2 * HD] * factor).astype(jnp.bfloat16)
+    for d in order:
+        rows = choose(picks[d], [fresh[0], fresh[1]])
+        if d == 0:
+            kv_fresh[0] = rows
+        else:
+            stage_fresh[d - 1] = rows
+            f_copies[d] = remote(
+                stage_fresh.at[d - 1], kv_fresh.at[d], f_send.at[d - 1], f_recv.at[d - 1],
+                {"docs": lax.rem(z + d, n_docs)},
+            )
+
+    for d in (1, 3, 2):
+        a_copies[d].wait_recv()
+        b_copies[d].wait_recv()
+        stored_step(d)
+    for d in (1, 3, 2):
+        f_copies[d].wait_recv()
+
+    source = lax.broadcasted_iota(jnp.int32, (1, n_docs * BLK), 1)
+    added = jnp.full((1, n_docs * BLK), bias[0], jnp.float32)
+    for d in range(1, n_docs):
+        added = jnp.where(source >= d * BLK, bias[d], added)
+    rows_all = n_docs * BLK
+    half_rows = GQA * half
+    heads_tile = tile // half
+    o_copy = None
+    for turn_of in range(2):
+        p = other if turn_of == 0 else s
+        for b in range(half_rows // tile):
+            at = pl.multiple_of(p * half_rows + b * tile, tile)
+            pages = kv_fresh[...].reshape(rows_all, 2 * HD)
+            top, row_sum, acc = step(at, pages[:, 0:HD], pages[:, HD : 2 * HD], added)
+            result = (acc / row_sum).astype(jnp.bfloat16)
+            for k in range(heads_tile):
+                piece = result[k * half : (k + 1) * half, :]
+                head = b * heads_tile + k
+                if turn_of == 0:
+                    o_send[:, head * HD : (head + 1) * HD] = piece
+                else:
+                    out_ref[:, lanes(s * GQA * HD + head * HD, HD)] = piece
+        if turn_of == 0:
+            o_copy = remote(o_send, out_ref.at[:, lanes(s * GQA * HD, GQA * HD)], o_sems.at[0], o_sems.at[1], partner)
+
+    for copy in chip + s_copies + p_copies:
+        copy.wait_send()
+    for d in range(1, n_docs):
+        a_copies[d].wait_send()
+        b_copies[d].wait_send()
+        f_copies[d].wait_send()
+    o_copy.wait()
+
+
+def fused(
+    hidden_rows, norm_gain, key_weight, value_weight, recompute_block, cache_keys, cache_values,
+    slot_of_doc, session_docs, session_count, turn_queries, turn_keys, turn_values, turn_length,
+):
+    width = hidden_rows.shape[-1]
+    half = QLEN // 2
+    rows = np.arange(4 * BLK, dtype=np.float64)[:, None]
+    angles = rows * ROPE_BASE ** (-np.arange(HD // 2, dtype=np.float64) * 2.0 / HD)[None, :]
+    cos_table = np.concatenate([np.cos(angles)] * 2, axis=1).astype(np.float32)
+    sin_table = np.concatenate([-np.sin(angles), np.sin(angles)], axis=1).astype(np.float32)
+    smem = pl.BlockSpec(memory_space=pltpu.SMEM)
+    vmem = pl.BlockSpec(memory_space=pltpu.VMEM)
+    hbm = pl.BlockSpec(memory_space=pltpu.HBM)
+    bf, f32 = jnp.bfloat16, jnp.float32
+    dma = pltpu.SemaphoreType.DMA
+    result = pl.pallas_call(
+        fused_kernel,
+        out_shape=jax.ShapeDtypeStruct((half, 2 * GQA * HD), bf),
+        in_specs=[smem] * 5 + [hbm, vmem] + [hbm] * 9,
+        out_specs=vmem,
+        scratch_shapes=[
+            pltpu.VMEM((2, BLK, width), bf),
+            pltpu.VMEM((2 * BLK, width), bf),
+            pltpu.VMEM((4, width, 2 * HD), bf),
+            pltpu.VMEM((2, 2 * BLK, 2 * HD), bf),
+            pltpu.VMEM((2, 2 * BLK, 2 * HD), bf),
+            pltpu.VMEM((2, half, 2 * HD), bf),
+            pltpu.VMEM((3, 3 * BLK, 2 * HD), bf),
+            pltpu.VMEM((4, 3 * BLK, 2 * HD), bf),
+            pltpu.VMEM((3, BLK, 2 * HD), bf),
+            pltpu.VMEM((4, BLK, 2 * HD), bf),
+            pltpu.VMEM((2, BLK, 2 * HD), bf),
+            pltpu.VMEM((4 * BLK, HD), f32),
+            pltpu.VMEM((4 * BLK, HD), f32),
+            pltpu.VMEM((3, 2 * BLK, 2 * HD), bf),
+            pltpu.VMEM((3, 2 * BLK, 2 * HD), bf),
+            pltpu.VMEM((2 * BLK, 2 * HD), f32),
+            pltpu.VMEM((8, BLK), f32),
+            pltpu.VMEM((3, 8, BLK), f32),
+            pltpu.VMEM((QLEN, GQA * HD), bf),
+            pltpu.VMEM((QLEN * GQA, HD), bf),
+            pltpu.VMEM((QLEN * GQA, 1), f32),
+            pltpu.VMEM((QLEN * GQA, 1), f32),
+            pltpu.VMEM((QLEN * GQA, HD), f32),
+            pltpu.VMEM((half, GQA * HD), bf),
+            dma((8,)), dma((8,)), dma((4,)), dma((4,)),
+            dma((3,)), dma((3,)), dma((3,)), dma((3,)), dma((3,)), dma((3,)),
+            dma((3,)), dma((3,)), dma((3,)), dma((3,)), dma((2,)),
+        ],
+        compiler_params=pltpu.CompilerParams(
+            collective_id=0, has_side_effects=True, vmem_limit_bytes=48 * 1024 * 1024
+        ),
+        cost_estimate=pl.CostEstimate(
+            flops=2_500_000_000, bytes_accessed=8_000_000, transcendentals=3_000_000
+        ),
+    )(
+        session_docs, session_count, slot_of_doc, recompute_block, turn_length,
+        hidden_rows, norm_gain.reshape(1, width), key_weight, value_weight, cache_keys, cache_values,
+        jnp.asarray(cos_table), jnp.asarray(sin_table), turn_queries, turn_keys, turn_values,
+    )
+    own_queries = lax.axis_index("sub") * half + jnp.arange(half, dtype=jnp.int32)
+    return jnp.where(own_queries[:, None] < turn_length[0], result, jnp.bfloat16(0.0))[None]
+
+
 def solution(mesh):
     in_specs = (
         P(("parts", "docs"), None, ("heads", "sub")),
@@ -208,4 +596,6 @@
         P(("parts", "docs")),
     )
     out_specs = P(("parts", "docs"), "sub", "heads")
-    return jax.shard_map(local, mesh=mesh, in_specs=in_specs, out_specs=out_specs, check_vma=False)
+    sizes = tuple(mesh.shape[name] for name in ("docs", "heads", "sub"))
+    chosen = fused if sizes == (4, 2, 2) else local
+    return jax.shard_map(chosen, mesh=mesh, in_specs=in_specs, out_specs=out_specs, check_vma=False)

time: 149 us -> 50 us (0.34)
  the two profiles are of different devices: /device:TPU:0 before, /device:TPU:17 now
where the time goes in v1:
time: 50 us; the launch traced here: 49.4 us
  Pallas kernels  35.4 us (71%)
  local copies, waits for them, and re-layouts  12.5 us (25%)
  other arithmetic  0.8 us (2%)
  between operations  0.69 us (1%)
    pallas_call x1, Pallas kernels, fused(): pl.pallas_call(fused_kernel, out_shape=jax.ShapeDtypeStruct((half, 2 * GQ...  35.4 us
    unnamed x26, local copies, waits for them, and re-layouts  11.8 us

profile of v1, /device:TPU:17, one launch (start us, length us, event | category | flops | bytes accessed | tf_op | source)
XLA Modules:
  0.0 49.4 jit_solution(9799290596267692193)
XLA Ops:
  0.7 0.7 %reshape.9.gain_ref = bf16[1,2048]{1,0:T(2,128)(2,1)S(1)} reshape(bf16[2048]{0:T(1024)(128)(2,1)} %param.17) | data formatting | bytes 8192 | tf_op jit(solution)/shard_map/reshape | solution.py:574
  1.3 0.0 copy-start
  1.3 1.6 %copy-done = bf16[2048,512]{1,0:T(8,128)(2,1)S(1)} copy-done((bf16[2048,512]{1,0:T(8,128)(2,1)S(1)}, bf16[2048,512]{1,0:T(8,128)(2,1)}, u32[]{:S(2)}) %copy-start) | copy-done | bytes 2097176
  2.9 0.0 copy-start.1
  2.9 1.2 %copy-done.1 = bf16[2,128,2048]{2,1,0:T(8,128)(2,1)S(1)} copy-done((bf16[2,128,2048]{2,1,0:T(8,128)(2,1)S(1)}, bf16[2,128,2048]{2,1,0:T(8,128)(2,1)}, u32[]{:S(2)}) %copy-start.1) | copy-done | bytes 1048600
  4.2 0.0 copy-start.2
  4.2 1.0 %copy-done.2 = bf16[1,128,2048]{2,1,0:T(8,128)(2,1)S(1)} copy-done((bf16[1,128,2048]{2,1,0:T(8,128)(2,1)S(1)}, bf16[1,128,2048]{2,1,0:T(8,128)(2,1)}, u32[]{:S(2)}) %copy-start.2) | copy-done | bytes 524312
  5.2 0.0 copy-start.3
  5.2 0.9 %copy-done.3 = bf16[2,256,256]{2,1,0:T(8,128)(2,1)S(1)} copy-done((bf16[2,256,256]{2,1,0:T(8,128)(2,1)S(1)}, bf16[2,256,256]{2,1,0:T(8,128)(2,1)}, u32[]{:S(2)}) %copy-start.3) | copy-done | bytes 262168
  6.2 0.9 %copy-done.4 = bf16[2,256,256]{2,1,0:T(8,128)(2,1)S(1)} copy-done((bf16[2,256,256]{2,1,0:T(8,128)(2,1)S(1)}, bf16[2,256,256]{2,1,0:T(8,128)(2,1)}, u32[]{:S(2)}) %copy-start.4) | copy-done | bytes 262168
  7.1 0.0 copy-start.5
  7.1 0.8 %copy-done.5 = bf16[1,64,256]{2,1,0:T(8,128)(2,1)S(1)} copy-done((bf16[1,64,256]{2,1,0:T(8,128)(2,1)S(1)}, bf16[1,64,256]{2,1,0:T(8,128)(2,1)}, u32[]{:S(2)}) %copy-start.5) | copy-done | bytes 32792
  7.9 0.0 copy-start.6
  7.9 0.8 %copy-done.6 = bf16[1,64,256]{2,1,0:T(8,128)(2,1)S(1)} copy-done((bf16[1,64,256]{2,1,0:T(8,128)(2,1)S(1)}, bf16[1,64,256]{2,1,0:T(8,128)(2,1)}, u32[]{:S(2)}) %copy-start.6) | copy-done | bytes 32792
  8.6 0.0 copy-start.7
  8.6 0.7 %copy-done.7 = s32[4,3]{1,0:T(4,128)S(1)} copy-done((s32[4,3]{1,0:T(4,128)S(1)}, s32[4,3]{1,0:T(4,128)}, u32[]{:S(2)}) %copy-start.7) | copy-done | bytes 72
  9.3 0.0 copy-start.8
  9.3 0.7 %copy-done.8 = s32[4]{0:T(128)S(1)} copy-done((s32[4]{0:T(128)S(1)}, s32[4]{0:T(128)}, u32[]{:S(2)}) %copy-start.8) | copy-done | bytes 40
  10.0 0.7 %copy-done.9 = s32[8]{0:T(128)S(1)} copy-done((s32[8]{0:T(128)S(1)}, s32[8]{0:T(128)}, u32[]{:S(2)}) %copy-start.9) | copy-done | bytes 56
  10.6 0.7 %copy-done.10 = s32[2]{0:T(128)S(1)} copy-done((s32[2]{0:T(128)S(1)}, s32[2]{0:T(128)}, u32[]{:S(2)}) %copy-start.10) | copy-done | bytes 32
  11.3 0.9 %copy-done.11 = f32[512,128]{1,0:T(8,128)S(1)} copy-done((f32[512,128]{1,0:T(8,128)S(1)}, f32[512,128]{1,0:T(8,128)}, u32[]{:S(2)}) %copy-start.11) | copy-done | bytes 262168
  12.2 0.9 %copy-done.12 = f32[512,128]{1,0:T(8,128)S(1)} copy-done((f32[512,128]{1,0:T(8,128)S(1)}, f32[512,128]{1,0:T(8,128)}, u32[]{:S(2)}) %copy-start.12) | copy-done | bytes 262168
  13.2 35.4 %shard_map.154 = bf16[64,2048]{1,0:T(8,128)(2,1)S(1)} custom-call(s32[4,3]{1,0:T(4,128)S(1)} %copy-done.7, s32[4]{0:T(128)S(1)} %copy-done.8, s32[8]{0:T(128)S(1)} %copy-done.9, s32[2]{0:T(128)S(1)} %copy-done.10, s32[1]{0:T(128)} %copy.17.length_sm, bf16[2,128,2048]{2,1,0:T(8,128)(2,1)S(1)} %copy-done.1, bf16[1,2048]{1,0:T(2,128)(2,1)S(1)} %reshape.9.gain_ref, ...), custom_call_target="tpu_custom_call" | custom-call | flops 2500000000 | bytes 8000000 | tf_op jit(solution)/shard_map/pallas_call | solution.py:532
  48.6 0.8 %select_bitcast_fusion = bf16[1,64,2048]{2,1,0:T(8,128)(2,1)} fusion(bf16[64,2048]{1,0:T(8,128)(2,1)S(1)} %shard_map.154, pred[64]{0:T(512)(128)(4,1)S(1)} %add_compare_fusion), kind=kLoop, calls=%fused_computation | loop fusion | flops 131072 | bytes 524352 | tf_op jit(solution)/shard_map/broadcast_in_dim | solution.py:578
  (6 shorter events, 0.0 us)
Async XLA Ops:
  1.3 1.6 %copy-start = (bf16[2048,512]{1,0:T(8,128)(2,1)S(1)}, bf16[2048,512]{1,0:T(8,128)(2,1)}, u32[]{:S(2)}) copy-start(bf16[2048,512]{1,0:T(8,128)(2,1)} %kw_hbm.1) | copy-start | bytes 6291460
  2.9 1.2 %copy-start.1 = (bf16[2,128,2048]{2,1,0:T(8,128)(2,1)S(1)}, bf16[2,128,2048]{2,1,0:T(8,128)(2,1)}, u32[]{:S(2)}) copy-start(bf16[2,128,2048]{2,1,0:T(8,128)(2,1)} %hidden_hbm.1) | copy-start | bytes 3145732
  4.2 1.0 %copy-start.2 = (bf16[1,128,2048]{2,1,0:T(8,128)(2,1)S(1)}, bf16[1,128,2048]{2,1,0:T(8,128)(2,1)}, u32[]{:S(2)}) copy-start(bf16[1,128,2048]{2,1,0:T(8,128)(2,1)} %tq_hbm.1) | copy-start | bytes 1572868
  5.2 0.9 %copy-start.3 = (bf16[2,256,256]{2,1,0:T(8,128)(2,1)S(1)}, bf16[2,256,256]{2,1,0:T(8,128)(2,1)}, u32[]{:S(2)}) copy-start(bf16[2,256,256]{2,1,0:T(8,128)(2,1)} %ck_hbm.1) | copy-start | bytes 786436
  6.2 0.9 %copy-start.4 = (bf16[2,256,256]{2,1,0:T(8,128)(2,1)S(1)}, bf16[2,256,256]{2,1,0:T(8,128)(2,1)}, u32[]{:S(2)}) copy-start(bf16[2,256,256]{2,1,0:T(8,128)(2,1)} %cv_hbm.1) | copy-start | bytes 786436
  7.1 0.8 %copy-start.5 = (bf16[1,64,256]{2,1,0:T(8,128)(2,1)S(1)}, bf16[1,64,256]{2,1,0:T(8,128)(2,1)}, u32[]{:S(2)}) copy-start(bf16[1,64,256]{2,1,0:T(8,128)(2,1)} %tk_hbm.1) | copy-start | bytes 98308
  7.9 0.8 %copy-start.6 = (bf16[1,64,256]{2,1,0:T(8,128)(2,1)S(1)}, bf16[1,64,256]{2,1,0:T(8,128)(2,1)}, u32[]{:S(2)}) copy-start(bf16[1,64,256]{2,1,0:T(8,128)(2,1)} %tv_hbm.1) | copy-start | bytes 98308
  8.6 0.7 %copy-start.7 = (s32[4,3]{1,0:T(4,128)S(1)}, s32[4,3]{1,0:T(4,128)}, u32[]{:S(2)}) copy-start(s32[4,3]{1,0:T(4,128)} %docs_sm.1) | copy-start | bytes 148
  9.3 0.7 %copy-start.8 = (s32[4]{0:T(128)S(1)}, s32[4]{0:T(128)}, u32[]{:S(2)}) copy-start(s32[4]{0:T(128)} %count_sm.1) | copy-start | bytes 52
  10.0 0.7 %copy-start.9 = (s32[8]{0:T(128)S(1)}, s32[8]{0:T(128)}, u32[]{:S(2)}) copy-start(s32[8]{0:T(128)} %slot_sm.1) | copy-start | bytes 100
  10.6 0.7 %copy-start.10 = (s32[2]{0:T(128)S(1)}, s32[2]{0:T(128)}, u32[]{:S(2)}) copy-start(s32[2]{0:T(128)} %block_sm.1) | copy-start | bytes 28
  11.3 0.9 %copy-start.11 = (f32[512,128]{1,0:T(8,128)S(1)}, f32[512,128]{1,0:T(8,128)}, u32[]{:S(2)}) copy-start(f32[512,128]{1,0:T(8,128)} %constant.12.clone.cos_hbm) | copy-start | bytes 786436
  12.2 0.9 %copy-start.12 = (f32[512,128]{1,0:T(8,128)S(1)}, f32[512,128]{1,0:T(8,128)}, u32[]{:S(2)}) copy-start(f32[512,128]{1,0:T(8,128)} %constant.13.clone.sin_hbm) | copy-start | bytes 786436

commit v2 on v1

--- a/solution.py
+++ b/solution.py
@@ -564,7 +564,7 @@
             dma((3,)), dma((3,)), dma((3,)), dma((3,)), dma((2,)),
         ],
         compiler_params=pltpu.CompilerParams(
-            collective_id=0, has_side_effects=True, vmem_limit_bytes=48 * 1024 * 1024
+            collective_id=0, has_side_effects=True, vmem_limit_bytes=63 * 1024 * 1024
         ),
         cost_estimate=pl.CostEstimate(
             flops=2_500_000_000, bytes_accessed=8_000_000, transcendentals=3_000_000

time: 50 us -> 39.8 us (0.80)
  the two profiles are of different devices: /device:TPU:17 before, /device:TPU:23 now
where the time goes in v2:
time: 39.8 us; the launch traced here: 39.6 us
  Pallas kernels  35.9 us (90%)
  other arithmetic  1.75 us (4%)
  local copies, waits for them, and re-layouts  1.29 us (3%)
  between operations  0.67 us (2%)
    pallas_call x1, Pallas kernels, fused(): pl.pallas_call(fused_kernel, out_shape=jax.ShapeDtypeStruct((half, 2 * GQ...  35.9 us
    broadcast_in_dim x1, other arithmetic, fused(): jnp.where(own_queries[:, None] < turn_length[0], result, jnp.bfloat16(0.0))  1.74 us
    reshape x1, local copies, waits for them, and re-layouts, fused(): norm_gain.reshape(1, width)  1.29 us

profile of v2, /device:TPU:23, one launch (start us, length us, event | category | flops | bytes accessed | tf_op | source)
XLA Modules:
  0.0 39.6 jit_solution(2781628328273635406)
XLA Ops:
  0.7 1.3 %reshape.9.gain_ref = bf16[1,2048]{1,0:T(2,128)(2,1)} reshape(bf16[2048]{0:T(1024)(128)(2,1)} %param.17) | data formatting | bytes 8192 | tf_op jit(solution)/shard_map/reshape | solution.py:574
  1.9 35.9 %shard_map.154 = bf16[64,2048]{1,0:T(8,128)(2,1)} custom-call(s32[4,3]{1,0:T(4,128)} %docs_sm.1, s32[4]{0:T(128)} %count_sm.1, s32[8]{0:T(128)} %slot_sm.1, s32[2]{0:T(128)} %block_sm.1, s32[1]{0:T(128)} %copy.17.length_sm, bf16[2,128,2048]{2,1,0:T(8,128)(2,1)} %hidden_hbm.1, bf16[1,2048]{1,0:T(2,128)(2,1)} %reshape.9.gain_ref, bf16[2048,512]{1,0:T(8,128)(2,1)} %kw_hbm.1, ...), custom_call_target="tpu_custom_call" | custom-call | flops 2500000000 | bytes 8000000 | tf_op jit(solution)/shard_map/pallas_call | solution.py:532
  37.8 1.7 %select_bitcast_fusion = bf16[1,64,2048]{2,1,0:T(8,128)(2,1)} fusion(bf16[64,2048]{1,0:T(8,128)(2,1)} %shard_map.154, pred[64]{0:T(512)(128)(4,1)S(1)} %add_compare_fusion), kind=kLoop, calls=%fused_computation | loop fusion | flops 131072 | bytes 524352 | tf_op jit(solution)/shard_map/broadcast_in_dim | solution.py:578
  (1 shorter events, 0.0 us)

commit v3 on v2

--- a/solution.py
+++ b/solution.py
@@ -209,12 +209,25 @@
     other = 1 - s
     mesh_id = pl.DeviceIdType.MESH
     pairs = [(1, 0), (1, 1), (0, 1), (0, 0)]
+    peers = [z, z + 1 - 2 * lax.rem(z, 2), lax.rem(z + 2, n_docs), 3 - z]
 
     def lanes(start, size):
         return pl.ds(pl.multiple_of(start, HD), size)
 
     my_cols = lanes(s * HD, HD)
     other_cols = lanes(other * HD, HD)
+
+    barrier = pltpu.get_barrier_semaphore()
+    for dh, ds in pairs[:3]:
+        pl.semaphore_signal(
+            barrier, inc=1,
+            device_id={"heads": lax.rem(h + dh, 2), "sub": lax.rem(s + ds, 2)},
+            device_id_type=mesh_id,
+        )
+    for d in range(1, n_docs):
+        pl.semaphore_signal(
+            barrier, inc=1, device_id={"docs": peers[d]}, device_id_type=mesh_id
+        )
 
     loads = [
         (ck_hbm.at[:, :, my_cols], own.at[:, :, 0:HD]),
@@ -248,19 +261,6 @@
     for i in range(3, len(loads)):
         loads[i].start()
 
-    barrier = pltpu.get_barrier_semaphore()
-    for dh, ds in pairs[:3]:
-        pl.semaphore_signal(
-            barrier, inc=1,
-            device_id={"heads": lax.rem(h + dh, 2), "sub": lax.rem(s + ds, 2)},
-            device_id_type=mesh_id,
-        )
-    for d in range(1, n_docs):
-        pl.semaphore_signal(
-            barrier, inc=1, device_id={"docs": lax.rem(z + d, n_docs)}, device_id_type=mesh_id
-        )
-    pl.semaphore_wait(barrier, 6)
-
     def remote(src, dst, send, recv, device):
         copy = pltpu.make_async_remote_copy(
             src_ref=src, dst_ref=dst, send_sem=send, recv_sem=recv,
@@ -268,14 +268,6 @@
         )
         copy.start()
         return copy
-
-    partner = {"sub": other}
-    chip = [
-        remote(ck_hbm.at[:, :, other_cols], oth.at[:, :, 0:HD], chip_send.at[0], chip_recv.at[0], partner),
-        remote(cv_hbm.at[:, :, other_cols], oth.at[:, :, HD : 2 * HD], chip_send.at[1], chip_recv.at[1], partner),
-        remote(tk_hbm.at[0, :, other_cols], turn.at[s, :, 0:HD], chip_send.at[2], chip_recv.at[2], partner),
-        remote(tv_hbm.at[0, :, other_cols], turn.at[s, :, HD : 2 * HD], chip_send.at[3], chip_recv.at[3], partner),
-    ]
 
     def reads(session, place):
         flag = jnp.int32(0)
@@ -292,10 +284,10 @@
             pick = jnp.where(hit, local_slot, pick)
         return flag, pick
 
-    picks = [reads(lax.rem(z + d, n_docs), z)[1] for d in range(n_docs)]
+    picks = [reads(peers[d], z)[1] for d in range(n_docs)]
     bias = []
     for d in range(n_docs):
-        flag, _ = reads(z, lax.rem(z + n_docs - d, n_docs))
+        flag, _ = reads(z, peers[d])
         bias.append(jnp.where(flag == 1, jnp.float32(0.0), jnp.float32(NEGATIVE)))
 
     def choose(index, blocks):
@@ -309,7 +301,7 @@
 
     loads[0].wait()
     loads[1].wait()
-    order = (2, 1, 3, 0)
+    order = (1, 2, 3, 0)
     holds, inner = [], []
     for d in range(n_docs):
         block = jnp.where(picks[d] == 1, block_sm[1], block_sm[0])
@@ -324,10 +316,21 @@
             kv[0, 0:BLK, :] = rows
         else:
             stage[d - 1, 0:BLK, :] = rows
-            a_copies[d] = remote(
-                stage.at[d - 1, 0:BLK], kv.at[d, 0:BLK], a_send.at[d - 1], a_recv.at[d - 1],
-                {"docs": lax.rem(z + d, n_docs)},
-            )
+    pl.semaphore_wait(barrier, 6)
+
+    partner = {"sub": other}
+    chip = [
+        remote(ck_hbm.at[:, :, other_cols], oth.at[:, :, 0:HD], chip_send.at[0], chip_recv.at[0], partner),
+        remote(cv_hbm.at[:, :, other_cols], oth.at[:, :, HD : 2 * HD], chip_send.at[1], chip_recv.at[1], partner),
+        remote(tk_hbm.at[0, :, other_cols], turn.at[s, :, 0:HD], chip_send.at[2], chip_recv.at[2], partner),
+        remote(tv_hbm.at[0, :, other_cols], turn.at[s, :, HD : 2 * HD], chip_send.at[3], chip_recv.at[3], partner),
+    ]
+
+    for d in (1, 2, 3):
+        a_copies[d] = remote(
+            stage.at[d - 1, 0:BLK], kv.at[d, 0:BLK], a_send.at[d - 1], a_recv.at[d - 1],
+            {"docs": peers[d]},
+        )
     chip[0].wait_recv()
     chip[1].wait_recv()
     for d in order:
@@ -345,12 +348,12 @@
             stage[d - 1, 2 * BLK : 3 * BLK, :] = third
             b_copies[d] = remote(
                 stage.at[d - 1, BLK : 3 * BLK], kv.at[d, BLK : 3 * BLK],
-                b_send.at[d - 1], b_recv.at[d - 1], {"docs": lax.rem(z + d, n_docs)},
+                b_send.at[d - 1], b_recv.at[d - 1], {"docs": peers[d]},
             )
 
     loads[2].wait()
     width = hid.shape[-1]
-    gain = gain_ref[...].astype(jnp.float32)
+    gain = gain_ref[...].astype(jnp.float32).reshape(1, width)
     sq_out[...] = jnp.zeros_like(sq_out)
     for j in range(2):
         total = jnp.zeros((BLK, HD), jnp.float32)
@@ -470,33 +473,38 @@
             stage_fresh[d - 1] = rows
             f_copies[d] = remote(
                 stage_fresh.at[d - 1], kv_fresh.at[d], f_send.at[d - 1], f_recv.at[d - 1],
-                {"docs": lax.rem(z + d, n_docs)},
+                {"docs": peers[d]},
             )
 
-    for d in (1, 3, 2):
+    for d in (1, 2, 3):
         a_copies[d].wait_recv()
         b_copies[d].wait_recv()
         stored_step(d)
-    for d in (1, 3, 2):
-        f_copies[d].wait_recv()
-
-    source = lax.broadcasted_iota(jnp.int32, (1, n_docs * BLK), 1)
-    added = jnp.full((1, n_docs * BLK), bias[0], jnp.float32)
-    for d in range(1, n_docs):
-        added = jnp.where(source >= d * BLK, bias[d], added)
-    rows_all = n_docs * BLK
+
+    def fresh_step(near, far):
+        page = kv_fresh[near : far + 1].reshape((far + 1 - near) * BLK, 2 * HD)
+        source = lax.broadcasted_iota(jnp.int32, (1, page.shape[0]), 1)
+        added = jnp.full((1, page.shape[0]), bias[near], jnp.float32)
+        for d in range(near + 1, far + 1):
+            added = jnp.where(source >= (d - near) * BLK, bias[d], added)
+        return page[:, 0:HD], page[:, HD : 2 * HD], added
+
+    f_copies[1].wait_recv()
+    f_copies[2].wait_recv()
+    f_copies[3].wait_recv()
     half_rows = GQA * half
     heads_tile = tile // half
     o_copy = None
     for turn_of in range(2):
         p = other if turn_of == 0 else s
+        query = lax.broadcasted_iota(jnp.int32, (half, HD), 0) + p * half
         for b in range(half_rows // tile):
             at = pl.multiple_of(p * half_rows + b * tile, tile)
-            pages = kv_fresh[...].reshape(rows_all, 2 * HD)
-            top, row_sum, acc = step(at, pages[:, 0:HD], pages[:, HD : 2 * HD], added)
-            result = (acc / row_sum).astype(jnp.bfloat16)
+            top, row_sum, acc = step(at, *fresh_step(0, 3))
+            result = acc * (1.0 / row_sum)
             for k in range(heads_tile):
-                piece = result[k * half : (k + 1) * half, :]
+                piece = jnp.where(query < length, result[k * half : (k + 1) * half, :], 0.0)
+                piece = piece.astype(jnp.bfloat16)
                 head = b * heads_tile + k
                 if turn_of == 0:
                     o_send[:, head * HD : (head + 1) * HD] = piece
@@ -571,11 +579,10 @@
         ),
     )(
         session_docs, session_count, slot_of_doc, recompute_block, turn_length,
-        hidden_rows, norm_gain.reshape(1, width), key_weight, value_weight, cache_keys, cache_values,
+        hidden_rows, norm_gain, key_weight, value_weight, cache_keys, cache_values,
         jnp.asarray(cos_table), jnp.asarray(sin_table), turn_queries, turn_keys, turn_values,
     )
-    own_queries = lax.axis_index("sub") * half + jnp.arange(half, dtype=jnp.int32)
-    return jnp.where(own_queries[:, None] < turn_length[0], result, jnp.bfloat16(0.0))[None]
+    return result[None]
 
 
 def solution(mesh):

time: 39.8 us -> 35 us (0.88)
  the two profiles are of different devices: /device:TPU:23 before, /device:TPU:0 now
where the time goes in v3:
time: 35 us; the launch traced here: 34.8 us
  Pallas kernels  32.5 us (93%)
  local copies, waits for them, and re-layouts  1.67 us (5%)
  between operations  0.66 us (2%)
    pallas_call x1, Pallas kernels, fused(): pl.pallas_call(fused_kernel, out_shape=jax.ShapeDtypeStruct((half, 2 * GQ...  32.5 us
    unnamed x1, local copies, waits for them, and re-layouts  1.67 us

profile of v3, /device:TPU:0, one launch (start us, length us, event | category | flops | bytes accessed | tf_op | source)
XLA Modules:
  0.0 34.8 jit_solution(13815346553693630608)
XLA Ops:
  0.7 32.5 %shard_map.154 = bf16[64,2048]{1,0:T(8,128)(2,1)} custom-call(s32[4,3]{1,0:T(4,128)} %docs_sm.1, s32[4]{0:T(128)} %count_sm.1, s32[8]{0:T(128)} %slot_sm.1, s32[2]{0:T(128)} %block_sm.1, s32[1]{0:T(128)S(6)} %copy.18.length_sm, bf16[2,128,2048]{2,1,0:T(8,128)(2,1)} %hidden_hbm.1, bf16[2048]{0:T(1024)(128)(2,1)} %gain_ref.1, bf16[2048,512]{1,0:T(8,128)(2,1)} %kw_hbm.1, ...), custom_call_target="tpu_custom_call" | custom-call | flops 2500000000 | bytes 8000000 | tf_op jit(solution)/shard_map/pallas_call | solution.py:540
  33.1 1.7 %copy.19 = bf16[1,64,2048]{2,1,0:T(8,128)(2,1)} copy(bf16[1,64,2048]{2,1,0:T(8,128)(2,1)} %bitcast.1) | data formatting | bytes 524288

commit v4 on v3

--- a/solution.py
+++ b/solution.py
@@ -16,6 +16,7 @@
 EPSILON = 1e-05
 ROPE_BASE = 500000.0
 NEGATIVE = -1e30
+LOG2_E = 1.4426950408889634
 
 
 def rotate(values, positions):
@@ -390,7 +391,7 @@
     chip[2].wait_recv()
     chip[3].wait_recv()
     length = length_sm[0]
-    scale = HD ** (-0.5)
+    scale = HD ** (-0.5) * LOG2_E
     tile = 256
 
     def scores_of(at, key_rows):
@@ -409,7 +410,7 @@
         seen = (key <= query) & (key < length)
         scores = jnp.where(seen, scores, NEGATIVE)
         top = jnp.max(scores, axis=-1, keepdims=True)
-        weights = jnp.exp(scores - top)
+        weights = jnp.exp2(scores - top)
         run_max[pl.ds(at, tile), :] = top
         run_sum[pl.ds(at, tile), :] = jnp.sum(weights, axis=-1, keepdims=True)
         run_acc[pl.ds(at, tile), :] = jnp.dot(
@@ -421,8 +422,8 @@
         scores = scores_of(at, key_rows) + added
         before = run_max[pl.ds(at, tile), :]
         top = jnp.maximum(before, jnp.max(scores, axis=-1, keepdims=True))
-        weights = jnp.exp(scores - top)
-        factor = jnp.exp(before - top)
+        weights = jnp.exp2(scores - top)
+        factor = jnp.exp2(before - top)
         row_sum = run_sum[pl.ds(at, tile), :] * factor + jnp.sum(weights, axis=-1, keepdims=True)
         acc = run_acc[pl.ds(at, tile), :] * factor + jnp.dot(
             weights.astype(jnp.bfloat16), value_rows, preferred_element_type=jnp.float32

time: 35 us -> 35 us (level)
  no operation moved by 1% of the time
where the time goes in v4:
time: 35 us; the launch traced here: 34.8 us
  Pallas kernels  32.4 us (93%)
  local copies, waits for them, and re-layouts  1.67 us (5%)
  between operations  0.66 us (2%)
    pallas_call x1, Pallas kernels, fused(): pl.pallas_call(fused_kernel, out_shape=jax.ShapeDtypeStruct((half, 2 * GQ...  32.4 us
    unnamed x1, local copies, waits for them, and re-layouts  1.67 us

profile of v4, /device:TPU:0, one launch (start us, length us, event | category | flops | bytes accessed | tf_op | source)
XLA Modules:
  0.0 34.8 jit_solution(6289931909808452964)
XLA Ops:
  0.7 32.4 %shard_map.154 = bf16[64,2048]{1,0:T(8,128)(2,1)} custom-call(s32[4,3]{1,0:T(4,128)} %docs_sm.1, s32[4]{0:T(128)} %count_sm.1, s32[8]{0:T(128)} %slot_sm.1, s32[2]{0:T(128)} %block_sm.1, s32[1]{0:T(128)S(6)} %copy.18.length_sm, bf16[2,128,2048]{2,1,0:T(8,128)(2,1)} %hidden_hbm.1, bf16[2048]{0:T(1024)(128)(2,1)} %gain_ref.1, bf16[2048,512]{1,0:T(8,128)(2,1)} %kw_hbm.1, ...), custom_call_target="tpu_custom_call" | custom-call | flops 2500000000 | bytes 8000000 | tf_op jit(solution)/shard_map/pallas_call | solution.py:541
  33.1 1.7 %copy.19 = bf16[1,64,2048]{2,1,0:T(8,128)(2,1)} copy(bf16[1,64,2048]{2,1,0:T(8,128)(2,1)} %bitcast.1) | data formatting | bytes 524288
